TPU v7x, 256 devices: a whole 4x4x8 slice. The times are simulated.
256 devices in a mesh: ctx: 128 (over z, x, y), head: 2 (over core).
Axes of the slice: x: 4, y: 4, z: 8, core: 2. Of those that a mesh axis runs over, the one named last changes fastest.
Arguments:
- queries: bfloat16 [65536, 512], P('ctx', 'head'), may hold values from -48 to 48
- keys: bfloat16 [65536, 128], P('ctx'), may hold values from -6 to 6
- values: bfloat16 [65536, 128], P('ctx'), may hold values from -6 to 6
- out_grad: bfloat16 [65536, 512], P('ctx', 'head'), may hold values from -6 to 6
- lengths: int32 [64], replicated, may hold values from 1 to 3584, 65536 in all
Outputs:
- attended: bfloat16 [65536, 512], P('ctx', 'head')
- query_grad: bfloat16 [65536, 512], P('ctx', 'head')
- key_grad: bfloat16 [65536, 128], P(('ctx', 'head'))
- value_grad: bfloat16 [65536, 128], P(('ctx', 'head'))
Inputs may be any that keep to these rules, and one draw needn't show every extreme that they name: The lengths sum to 65536, and the largest is exactly 3584.
All inputs are finite; a program needn't handle non-finite values.
Results may differ from a plain program's by a relative error of at most 0.038.
Values may be sent and summed in bfloat16 or wider, within the bound.
A program may use at most 128 MiB of HBM per device.

v0:
```python
import math

import jax
import jax.numpy as jnp
from jax import lax
from jax.sharding import PartitionSpec as P

WIN = 8


neg_big = -1e30


def from_behind(block, axis, distance):
    devices = range(lax.axis_size(axis))
    route = [(i - distance, i) for i in devices if i - distance in devices]
    return lax.ppermute(block, axis, route)


def doc_begin(lengths, positions):
    ends = jnp.cumsum(lengths)
    begins = ends - lengths
    inside = begins[None, :] <= positions[:, None]
    return jnp.max(jnp.where(inside, begins[None, :], 0), axis=1)


def masked_scores(query_heads, block_keys, query_pos, query_begin, key_first, score_scale):
    scores = (
        jnp.einsum("rhd,cd->hrc", query_heads, block_keys, preferred_element_type=jnp.float32)
        * score_scale
    )
    key_pos = key_first + jnp.arange(block_keys.shape[0], dtype=jnp.int32)
    allowed = (key_pos[None, :] >= query_begin[:, None]) & (key_pos[None, :] <= query_pos[:, None])
    return jnp.where(allowed[None], scores, neg_big)


def kv_window(keys, values):
    joined = jnp.stack([keys, values])
    block_list = [joined]
    current = joined
    for distance in range(1, WIN):
        current = from_behind(current, "ctx", 1)
        block_list.append(current)
    return jnp.stack(block_list)


def return_partials(partials):
    summed = partials[WIN - 1]
    for distance in range(WIN - 2, -1, -1):
        summed = (
            from_behind(summed.astype(jnp.bfloat16), "ctx", -1).astype(summed.dtype)
            + partials[distance]
        )
    return summed


def block_pass(
    query_heads, grad_heads, query_pos, query_begin, block_list, key_firsts, score_scale
):
    row_count, head_count, head_width = query_heads.shape
    row_max = jnp.full((head_count, row_count), neg_big, jnp.float32)
    row_sum = jnp.zeros((head_count, row_count), jnp.float32)
    for index in range(len(block_list)):
        block_keys = block_list[index][0]
        key_first = key_firsts[index]
        old_max = row_max
        old_sum = row_sum
        scores = masked_scores(
            query_heads, block_keys, query_pos, query_begin, key_first, score_scale
        )
        new_max = jnp.maximum(old_max, jnp.max(scores, axis=-1))
        new_sum = old_sum * jnp.exp(old_max - new_max) + jnp.sum(
            jnp.exp(scores - new_max[:, :, None]), axis=-1
        )
        row_max = new_max
        row_sum = new_sum
    log_total = row_max + jnp.log(row_sum)
    attended_sum = jnp.zeros((row_count, head_count, head_width), jnp.float32)
    for index in range(len(block_list)):
        block_keys, block_values = block_list[index]
        key_first = key_firsts[index]
        add_scores = masked_scores(
            query_heads, block_keys, query_pos, query_begin, key_first, score_scale
        )
        weights_low = jnp.exp(add_scores - log_total[:, :, None]).astype(jnp.bfloat16)
        attended_sum = attended_sum + jnp.einsum(
            "hrc,cd->rhd", weights_low, block_values, preferred_element_type=jnp.float32
        )
    attended = attended_sum.astype(jnp.bfloat16)
    row_delta = jnp.sum(grad_heads.astype(jnp.float32) * attended.astype(jnp.float32), axis=-1).T
    query_sum = jnp.zeros((row_count, head_count, head_width), jnp.float32)
    partial_list = []
    for index in range(len(block_list)):
        block_keys, block_values = block_list[index]
        key_first = key_firsts[index]
        back_scores = masked_scores(
            query_heads, block_keys, query_pos, query_begin, key_first, score_scale
        )
        prob_full = jnp.exp(back_scores - log_total[:, :, None])
        prob_low = prob_full.astype(jnp.bfloat16)
        prob_grad = jnp.einsum(
            "rhd,cd->hrc", grad_heads, block_values, preferred_element_type=jnp.float32
        )
        score_grad = (prob_full * (prob_grad - row_delta[:, :, None])).astype(jnp.bfloat16)
        new_query = (
            query_sum
            + jnp.einsum("hrc,cd->rhd", score_grad, block_keys, preferred_element_type=jnp.float32)
            * score_scale
        )
        key_part = (
            jnp.einsum("hrc,rhd->cd", score_grad, query_heads, preferred_element_type=jnp.float32)
            * score_scale
        )
        value_part = jnp.einsum(
            "hrc,rhd->cd", prob_low, grad_heads, preferred_element_type=jnp.float32
        )
        query_sum = new_query
        block_part = jnp.stack([key_part, value_part])
        partial_list.append(block_part)
    return (attended, query_sum.astype(jnp.bfloat16), jnp.stack(partial_list))


def on_device(queries, keys, values, out_grad, lengths):
    tok_rows = keys.shape[0]
    head_width = keys.shape[1]
    head_count = queries.shape[1] // head_width
    score_scale = 1.0 / math.sqrt(head_width)
    my_rank = lax.axis_index("ctx")
    query_pos = my_rank * tok_rows + jnp.arange(tok_rows, dtype=jnp.int32)
    query_begin = doc_begin(lengths, query_pos)
    query_heads = queries.reshape(tok_rows, head_count, head_width)
    grad_heads = out_grad.reshape(tok_rows, head_count, head_width)
    window = kv_window(keys, values)
    block_list = [(window[distance, 0], window[distance, 1]) for distance in range(WIN)]
    key_firsts = [(my_rank - distance) * tok_rows for distance in range(WIN)]
    attended, query_low, partials = block_pass(
        query_heads, grad_heads, query_pos, query_begin, block_list, key_firsts, score_scale
    )
    owned = lax.psum_scatter(
        return_partials(partials).astype(jnp.bfloat16), "head", scatter_dimension=1, tiled=True
    ).astype(jnp.float32)
    attended_out = attended.reshape(tok_rows, head_count * head_width)
    query_out = query_low.reshape(tok_rows, head_count * head_width)
    return (attended_out, query_out, owned[0].astype(jnp.bfloat16), owned[1].astype(jnp.bfloat16))


def solution(mesh):
    placed = (P("ctx", "head"), P("ctx", None), P("ctx", None), P("ctx", "head"), P())
    return jax.shard_map(
        on_device,
        mesh=mesh,
        in_specs=placed,
        out_specs=(
            P("ctx", "head"),
            P("ctx", "head"),
            P(("ctx", "head"), None),
            P(("ctx", "head"), None),
        ),
        check_vma=False,
    )
```

profile of v0, /device:TPU:97, one launch (start us, length us, event | category | flops | bytes accessed | tf_op | source)
XLA Modules:
  0.0 241.8 jit_solution(14855114579587058383)
XLA Ops:
  8.3 3.2 %collective-permute-start = (bf16[2,512,128]{2,1,0:T(8,128)(2,1)S(1)}, bf16[2,512,128]{2,1,0:T(8,128)(2,1)S(1)}, u32[]{:S(2)}, u32[]{:S(2)}) collective-permute-start(bf16[2,512,128]{2,1,0:T(8,128)(2,1)S(1)} %get-tuple-element.23), channel_id=1, source_target_pairs={{0,2},{2,4},{4,6},{6,8},{8,10},{10,12},{12,14},{14,16},{16,18},{18... | collective-permute-start | bytes 786440 | tf_op jit(solution)/shard_map/ppermute | solution.py:17
  14.3 2.0 compare_and_fusion.6
  16.9 4.7 %collective-permute-done = bf16[2,512,128]{2,1,0:T(8,128)(2,1)S(1)} collective-permute-done((bf16[2,512,128]{2,1,0:T(8,128)(2,1)S(1)}, bf16[2,512,128]{2,1,0:T(8,128)(2,1)S(1)}, u32[]{:S(2)}, u32[]{:S(2)}) %collective-permute-start) | collective-permute-done | bytes 262176 | tf_op jit(solution)/shard_map/ppermute | solution.py:17
  24.0 9.9 %collective-permute-done.1 = bf16[2,512,128]{2,1,0:T(8,128)(2,1)S(1)} collective-permute-done((bf16[2,512,128]{2,1,0:T(8,128)(2,1)S(1)}, bf16[2,512,128]{2,1,0:T(8,128)(2,1)S(1)}, u32[]{:S(2)}, u32[]{:S(2)}) %collective-permute-start.1) | collective-permute-done | bytes 262176 | tf_op jit(solution)/shard_map/ppermute | solution.py:17
  36.4 8.8 %collective-permute-done.2 = bf16[2,512,128]{2,1,0:T(8,128)(2,1)S(1)} collective-permute-done((bf16[2,512,128]{2,1,0:T(8,128)(2,1)S(1)}, bf16[2,512,128]{2,1,0:T(8,128)(2,1)S(1)}, u32[]{:S(2)}, u32[]{:S(2)}) %collective-permute-start.2) | collective-permute-done | bytes 262176 | tf_op jit(solution)/shard_map/ppermute | solution.py:17
  47.7 8.8 %collective-permute-done.3 = bf16[2,512,128]{2,1,0:T(8,128)(2,1)S(1)} collective-permute-done((bf16[2,512,128]{2,1,0:T(8,128)(2,1)S(1)}, bf16[2,512,128]{2,1,0:T(8,128)(2,1)S(1)}, u32[]{:S(2)}, u32[]{:S(2)}) %collective-permute-start.3) | collective-permute-done | bytes 262176 | tf_op jit(solution)/shard_map/ppermute | solution.py:17
  59.0 8.8 %collective-permute-done.4 = bf16[2,512,128]{2,1,0:T(8,128)(2,1)S(1)} collective-permute-done((bf16[2,512,128]{2,1,0:T(8,128)(2,1)S(1)}, bf16[2,512,128]{2,1,0:T(8,128)(2,1)S(1)}, u32[]{:S(2)}, u32[]{:S(2)}) %collective-permute-start.4) | collective-permute-done | bytes 262176 | tf_op jit(solution)/shard_map/ppermute | solution.py:17
  70.4 8.8 %collective-permute-done.5 = bf16[2,512,128]{2,1,0:T(8,128)(2,1)S(1)} collective-permute-done((bf16[2,512,128]{2,1,0:T(8,128)(2,1)S(1)}, bf16[2,512,128]{2,1,0:T(8,128)(2,1)S(1)}, u32[]{:S(2)}, u32[]{:S(2)}) %collective-permute-start.5) | collective-permute-done | bytes 262176 | tf_op jit(solution)/shard_map/ppermute | solution.py:17
  79.2 2.1 collective-permute-start.6
  81.9 8.7 %collective-permute-done.6 = bf16[2,512,128]{2,1,0:T(8,128)(2,1)S(1)} collective-permute-done((bf16[2,512,128]{2,1,0:T(8,128)(2,1)S(1)}, bf16[2,512,128]{2,1,0:T(8,128)(2,1)S(1)}, u32[]{:S(2)}, u32[]{:S(2)}) %collective-permute-start.6) | collective-permute-done | bytes 262176 | tf_op jit(solution)/shard_map/ppermute | solution.py:17
  105.6 1.9 collective-permute-start.7
  112.8 6.1 %collective-permute-start.8 = (bf16[2,512,128]{2,1,0:T(8,128)(2,1)S(1)}, bf16[2,512,128]{2,1,0:T(8,128)(2,1)S(1)}, u32[]{:S(2)}, u32[]{:S(2)}) collective-permute-start(bf16[2,512,128]{2,1,0:T(8,128)(2,1)S(1)} %fusion.46), channel_id=1, source_target_pairs={{2,0},{4,2},{6,4},{8,6},{10,8},{12,10},{14,12},{16,14},{18,16},{20... | collective-permute-start | bytes 786440 | tf_op jit(solution)/shard_map/ppermute | solution.py:17
  119.3 3.0 %collective-permute-done.8 = bf16[2,512,128]{2,1,0:T(8,128)(2,1)S(1)} collective-permute-done((bf16[2,512,128]{2,1,0:T(8,128)(2,1)S(1)}, bf16[2,512,128]{2,1,0:T(8,128)(2,1)S(1)}, u32[]{:S(2)}, u32[]{:S(2)}) %collective-permute-start.8) | collective-permute-done | bytes 262176 | tf_op jit(solution)/shard_map/ppermute | solution.py:17
  122.3 8.0 %collective-permute-start.9 = (bf16[2,512,128]{2,1,0:T(8,128)(2,1)S(1)}, bf16[2,512,128]{2,1,0:T(8,128)(2,1)S(1)}, u32[]{:S(2)}, u32[]{:S(2)}) collective-permute-start(bf16[2,512,128]{2,1,0:T(8,128)(2,1)S(1)} %fusion.47), channel_id=1, source_target_pairs={{2,0},{4,2},{6,4},{8,6},{10,8},{12,10},{14,12},{16,14},{18,16},{20... | collective-permute-start | bytes 786440 | tf_op jit(solution)/shard_map/ppermute | solution.py:17
  130.7 3.9 %collective-permute-done.9 = bf16[2,512,128]{2,1,0:T(8,128)(2,1)S(1)} collective-permute-done((bf16[2,512,128]{2,1,0:T(8,128)(2,1)S(1)}, bf16[2,512,128]{2,1,0:T(8,128)(2,1)S(1)}, u32[]{:S(2)}, u32[]{:S(2)}) %collective-permute-start.9) | collective-permute-done | bytes 262176 | tf_op jit(solution)/shard_map/ppermute | solution.py:17
  134.6 8.0 %collective-permute-start.10 = (bf16[2,512,128]{2,1,0:T(8,128)(2,1)S(1)}, bf16[2,512,128]{2,1,0:T(8,128)(2,1)S(1)}, u32[]{:S(2)}, u32[]{:S(2)}) collective-permute-start(bf16[2,512,128]{2,1,0:T(8,128)(2,1)S(1)} %fusion.48), channel_id=1, source_target_pairs={{2,0},{4,2},{6,4},{8,6},{10,8},{12,10},{14,12},{16,14},{18,16},{20... | collective-permute-start | bytes 786440 | tf_op jit(solution)/shard_map/ppermute | solution.py:17
  143.0 4.9 %collective-permute-done.10 = bf16[2,512,128]{2,1,0:T(8,128)(2,1)S(1)} collective-permute-done((bf16[2,512,128]{2,1,0:T(8,128)(2,1)S(1)}, bf16[2,512,128]{2,1,0:T(8,128)(2,1)S(1)}, u32[]{:S(2)}, u32[]{:S(2)}) %collective-permute-start.10) | collective-permute-done | bytes 262176 | tf_op jit(solution)/shard_map/ppermute | solution.py:17
  148.0 8.0 %collective-permute-start.11 = (bf16[2,512,128]{2,1,0:T(8,128)(2,1)S(1)}, bf16[2,512,128]{2,1,0:T(8,128)(2,1)S(1)}, u32[]{:S(2)}, u32[]{:S(2)}) collective-permute-start(bf16[2,512,128]{2,1,0:T(8,128)(2,1)S(1)} %fusion.49), channel_id=1, source_target_pairs={{2,0},{4,2},{6,4},{8,6},{10,8},{12,10},{14,12},{16,14},{18,16},{20... | collective-permute-start | bytes 786440 | tf_op jit(solution)/shard_map/ppermute | solution.py:17
  156.4 5.5 %collective-permute-done.11 = bf16[2,512,128]{2,1,0:T(8,128)(2,1)S(1)} collective-permute-done((bf16[2,512,128]{2,1,0:T(8,128)(2,1)S(1)}, bf16[2,512,128]{2,1,0:T(8,128)(2,1)S(1)}, u32[]{:S(2)}, u32[]{:S(2)}) %collective-permute-start.11) | collective-permute-done | bytes 262176 | tf_op jit(solution)/shard_map/ppermute | solution.py:17
  161.9 8.3 %collective-permute-start.12 = (bf16[2,512,128]{2,1,0:T(8,128)(2,1)S(1)}, bf16[2,512,128]{2,1,0:T(8,128)(2,1)S(1)}, u32[]{:S(2)}, u32[]{:S(2)}) collective-permute-start(bf16[2,512,128]{2,1,0:T(8,128)(2,1)S(1)} %fusion.50), channel_id=1, source_target_pairs={{2,0},{4,2},{6,4},{8,6},{10,8},{12,10},{14,12},{16,14},{18,16},{20... | collective-permute-start | bytes 786440 | tf_op jit(solution)/shard_map/ppermute | solution.py:17
  170.6 4.6 %collective-permute-done.12 = bf16[2,512,128]{2,1,0:T(8,128)(2,1)S(1)} collective-permute-done((bf16[2,512,128]{2,1,0:T(8,128)(2,1)S(1)}, bf16[2,512,128]{2,1,0:T(8,128)(2,1)S(1)}, u32[]{:S(2)}, u32[]{:S(2)}) %collective-permute-start.12) | collective-permute-done | bytes 262176 | tf_op jit(solution)/shard_map/ppermute | solution.py:17
  175.3 8.3 %collective-permute-start.13 = (bf16[2,512,128]{2,1,0:T(8,128)(2,1)S(1)}, bf16[2,512,128]{2,1,0:T(8,128)(2,1)S(1)}, u32[]{:S(2)}, u32[]{:S(2)}) collective-permute-start(bf16[2,512,128]{2,1,0:T(8,128)(2,1)S(1)} %fusion.51), channel_id=1, source_target_pairs={{2,0},{4,2},{6,4},{8,6},{10,8},{12,10},{14,12},{16,14},{18,16},{20... | collective-permute-start | bytes 786440 | tf_op jit(solution)/shard_map/ppermute | solution.py:17
  184.0 3.7 %collective-permute-done.13 = bf16[2,512,128]{2,1,0:T(8,128)(2,1)S(1)} collective-permute-done((bf16[2,512,128]{2,1,0:T(8,128)(2,1)S(1)}, bf16[2,512,128]{2,1,0:T(8,128)(2,1)S(1)}, u32[]{:S(2)}, u32[]{:S(2)}) %collective-permute-start.13) | collective-permute-done | bytes 262176 | tf_op jit(solution)/shard_map/ppermute | solution.py:17
  191.4 42.0 %reduce-scatter.2.cloned.1.call-done = bf16[2,256,128]{2,1,0:T(8,128)(2,1)} async-done(((bf16[2,512,128]{2,1,0:T(8,128)(2,1)}), bf16[2,256,128]{2,1,0:T(8,128)(2,1)}) %reduce-scatter.2.cloned.1.call-update) | async-done | bytes 131088 | tf_op jit(solution)/shard_map/reduce_scatter | solution.py:139
  (102 shorter events, 44.9 us)
Async XLA Ops:
  7.2 9.2 %copy-start = (bf16[512,256]{1,0:T(8,128)(2,1)S(1)}, bf16[512,256]{1,0:T(8,128)(2,1)}, u32[]{:S(2)}) copy-start(bf16[512,256]{1,0:T(8,128)(2,1)} %param.5) | copy-start | bytes 786436
  7.2 226.3 %reduce-scatter.2.cloned.1.call-start = ((), (), s32[]{:S(2)}) async-start(), calls=%async_computation.1 | async-start | bytes 393216 | tf_op jit(solution)/shard_map/reduce_scatter | solution.py:139
  8.3 13.3 %collective-permute-start = (bf16[2,512,128]{2,1,0:T(8,128)(2,1)S(1)}, bf16[2,512,128]{2,1,0:T(8,128)(2,1)S(1)}, u32[]{:S(2)}, u32[]{:S(2)}) collective-permute-start(bf16[2,512,128]{2,1,0:T(8,128)(2,1)S(1)} %get-tuple-element.23), channel_id=1, source_target_pairs={{0,2},{2,4},{4,6},{6,8},{8,10},{10,12},{12,14},{14,16},{16,18},{18... | collective-permute-start | bytes 786440 | tf_op jit(solution)/shard_map/ppermute | solution.py:17
  21.6 81.9 %copy-start.1 = (bf16[2,512,128]{2,1,0:T(8,128)(2,1)}, bf16[2,512,128]{2,1,0:T(8,128)(2,1)S(1)}, u32[]{:S(2)}) copy-start(bf16[2,512,128]{2,1,0:T(8,128)(2,1)S(1)} %collective-permute-done) | copy-start | bytes 786436
  21.6 12.4 %collective-permute-start.1 = (bf16[2,512,128]{2,1,0:T(8,128)(2,1)S(1)}, bf16[2,512,128]{2,1,0:T(8,128)(2,1)S(1)}, u32[]{:S(2)}, u32[]{:S(2)}) collective-permute-start(bf16[2,512,128]{2,1,0:T(8,128)(2,1)S(1)} %collective-permute-done), channel_id=1, source_target_pairs={{0,2},{2,4},{4,6},{6,8},{8,10},{10,12},{12,14},{14,16},{16,18},{18... | collective-permute-start | bytes 786440 | tf_op jit(solution)/shard_map/ppermute | solution.py:17
  33.9 11.3 %collective-permute-start.2 = (bf16[2,512,128]{2,1,0:T(8,128)(2,1)S(1)}, bf16[2,512,128]{2,1,0:T(8,128)(2,1)S(1)}, u32[]{:S(2)}, u32[]{:S(2)}) collective-permute-start(bf16[2,512,128]{2,1,0:T(8,128)(2,1)S(1)} %collective-permute-done.1), channel_id=1, source_target_pairs={{0,2},{2,4},{4,6},{6,8},{8,10},{10,12},{12,14},{14,16},{16,18},{18... | collective-permute-start | bytes 786440 | tf_op jit(solution)/shard_map/ppermute | solution.py:17
  45.2 11.3 %collective-permute-start.3 = (bf16[2,512,128]{2,1,0:T(8,128)(2,1)S(1)}, bf16[2,512,128]{2,1,0:T(8,128)(2,1)S(1)}, u32[]{:S(2)}, u32[]{:S(2)}) collective-permute-start(bf16[2,512,128]{2,1,0:T(8,128)(2,1)S(1)} %collective-permute-done.2), channel_id=1, source_target_pairs={{0,2},{2,4},{4,6},{6,8},{8,10},{10,12},{12,14},{14,16},{16,18},{18... | collective-permute-start | bytes 786440 | tf_op jit(solution)/shard_map/ppermute | solution.py:17
  56.6 11.3 %collective-permute-start.4 = (bf16[2,512,128]{2,1,0:T(8,128)(2,1)S(1)}, bf16[2,512,128]{2,1,0:T(8,128)(2,1)S(1)}, u32[]{:S(2)}, u32[]{:S(2)}) collective-permute-start(bf16[2,512,128]{2,1,0:T(8,128)(2,1)S(1)} %collective-permute-done.3), channel_id=1, source_target_pairs={{0,2},{2,4},{4,6},{6,8},{8,10},{10,12},{12,14},{14,16},{16,18},{18... | collective-permute-start | bytes 786440 | tf_op jit(solution)/shard_map/ppermute | solution.py:17
  67.9 11.3 %collective-permute-start.5 = (bf16[2,512,128]{2,1,0:T(8,128)(2,1)S(1)}, bf16[2,512,128]{2,1,0:T(8,128)(2,1)S(1)}, u32[]{:S(2)}, u32[]{:S(2)}) collective-permute-start(bf16[2,512,128]{2,1,0:T(8,128)(2,1)S(1)} %collective-permute-done.4), channel_id=1, source_target_pairs={{0,2},{2,4},{4,6},{6,8},{8,10},{10,12},{12,14},{14,16},{16,18},{18... | collective-permute-start | bytes 786440 | tf_op jit(solution)/shard_map/ppermute | solution.py:17
  79.2 19.5 %copy-start.3 = (bf16[2,512,128]{2,1,0:T(8,128)(2,1)}, bf16[2,512,128]{2,1,0:T(8,128)(2,1)S(1)}, u32[]{:S(2)}) copy-start(bf16[2,512,128]{2,1,0:T(8,128)(2,1)S(1)} %collective-permute-done.5) | copy-start | bytes 786436
  79.2 11.3 %collective-permute-start.6 = (bf16[2,512,128]{2,1,0:T(8,128)(2,1)S(1)}, bf16[2,512,128]{2,1,0:T(8,128)(2,1)S(1)}, u32[]{:S(2)}, u32[]{:S(2)}) collective-permute-start(bf16[2,512,128]{2,1,0:T(8,128)(2,1)S(1)} %collective-permute-done.5), channel_id=1, source_target_pairs={{0,2},{2,4},{4,6},{6,8},{8,10},{10,12},{12,14},{14,16},{16,18},{18... | collective-permute-start | bytes 786440 | tf_op jit(solution)/shard_map/ppermute | solution.py:17
  90.5 7.6 %copy-start.5 = (bf16[2,512,128]{2,1,0:T(8,128)(2,1)}, bf16[2,512,128]{2,1,0:T(8,128)(2,1)S(1)}, u32[]{:S(2)}) copy-start(bf16[2,512,128]{2,1,0:T(8,128)(2,1)S(1)} %collective-permute-done.6) | copy-start | bytes 786436
  105.6 7.1 %collective-permute-start.7 = (bf16[2,512,128]{2,1,0:T(8,128)(2,1)S(1)}, bf16[2,512,128]{2,1,0:T(8,128)(2,1)S(1)}, u32[]{:S(2)}, u32[]{:S(2)}) collective-permute-start(bf16[2,512,128]{2,1,0:T(8,128)(2,1)S(1)} %pad_maximum_fusion.1), channel_id=1, source_target_pairs={{2,0},{4,2},{6,4},{8,6},{10,8},{12,10},{14,12},{16,14},{18,16},{20... | collective-permute-start | bytes 786440 | tf_op jit(solution)/shard_map/ppermute | solution.py:17
  111.1 19.3 %copy-start.2 = (bf16[2,512,128]{2,1,0:T(8,128)(2,1)S(1)}, bf16[2,512,128]{2,1,0:T(8,128)(2,1)}, u32[]{:S(2)}) copy-start(bf16[2,512,128]{2,1,0:T(8,128)(2,1)} %copy-done.1) | copy-start | bytes 786436
  112.8 9.4 %collective-permute-start.8 = (bf16[2,512,128]{2,1,0:T(8,128)(2,1)S(1)}, bf16[2,512,128]{2,1,0:T(8,128)(2,1)S(1)}, u32[]{:S(2)}, u32[]{:S(2)}) collective-permute-start(bf16[2,512,128]{2,1,0:T(8,128)(2,1)S(1)} %fusion.46), channel_id=1, source_target_pairs={{2,0},{4,2},{6,4},{8,6},{10,8},{12,10},{14,12},{16,14},{18,16},{20... | collective-permute-start | bytes 786440 | tf_op jit(solution)/shard_map/ppermute | solution.py:17
  122.3 12.2 %collective-permute-start.9 = (bf16[2,512,128]{2,1,0:T(8,128)(2,1)S(1)}, bf16[2,512,128]{2,1,0:T(8,128)(2,1)S(1)}, u32[]{:S(2)}, u32[]{:S(2)}) collective-permute-start(bf16[2,512,128]{2,1,0:T(8,128)(2,1)S(1)} %fusion.47), channel_id=1, source_target_pairs={{2,0},{4,2},{6,4},{8,6},{10,8},{12,10},{14,12},{16,14},{18,16},{20... | collective-permute-start | bytes 786440 | tf_op jit(solution)/shard_map/ppermute | solution.py:17
  134.6 13.3 %collective-permute-start.10 = (bf16[2,512,128]{2,1,0:T(8,128)(2,1)S(1)}, bf16[2,512,128]{2,1,0:T(8,128)(2,1)S(1)}, u32[]{:S(2)}, u32[]{:S(2)}) collective-permute-start(bf16[2,512,128]{2,1,0:T(8,128)(2,1)S(1)} %fusion.48), channel_id=1, source_target_pairs={{2,0},{4,2},{6,4},{8,6},{10,8},{12,10},{14,12},{16,14},{18,16},{20... | collective-permute-start | bytes 786440 | tf_op jit(solution)/shard_map/ppermute | solution.py:17
  148.0 13.9 %collective-permute-start.11 = (bf16[2,512,128]{2,1,0:T(8,128)(2,1)S(1)}, bf16[2,512,128]{2,1,0:T(8,128)(2,1)S(1)}, u32[]{:S(2)}, u32[]{:S(2)}) collective-permute-start(bf16[2,512,128]{2,1,0:T(8,128)(2,1)S(1)} %fusion.49), channel_id=1, source_target_pairs={{2,0},{4,2},{6,4},{8,6},{10,8},{12,10},{14,12},{16,14},{18,16},{20... | collective-permute-start | bytes 786440 | tf_op jit(solution)/shard_map/ppermute | solution.py:17
  161.9 13.3 %collective-permute-start.12 = (bf16[2,512,128]{2,1,0:T(8,128)(2,1)S(1)}, bf16[2,512,128]{2,1,0:T(8,128)(2,1)S(1)}, u32[]{:S(2)}, u32[]{:S(2)}) collective-permute-start(bf16[2,512,128]{2,1,0:T(8,128)(2,1)S(1)} %fusion.50), channel_id=1, source_target_pairs={{2,0},{4,2},{6,4},{8,6},{10,8},{12,10},{14,12},{16,14},{18,16},{20... | collective-permute-start | bytes 786440 | tf_op jit(solution)/shard_map/ppermute | solution.py:17
  170.6 17.9 %copy-start.4 = (bf16[2,512,128]{2,1,0:T(8,128)(2,1)S(1)}, bf16[2,512,128]{2,1,0:T(8,128)(2,1)}, u32[]{:S(2)}) copy-start(bf16[2,512,128]{2,1,0:T(8,128)(2,1)} %copy-done.3) | copy-start | bytes 786436
  175.3 12.4 %collective-permute-start.13 = (bf16[2,512,128]{2,1,0:T(8,128)(2,1)S(1)}, bf16[2,512,128]{2,1,0:T(8,128)(2,1)S(1)}, u32[]{:S(2)}, u32[]{:S(2)}) collective-permute-start(bf16[2,512,128]{2,1,0:T(8,128)(2,1)S(1)} %fusion.51), channel_id=1, source_target_pairs={{2,0},{4,2},{6,4},{8,6},{10,8},{12,10},{14,12},{16,14},{18,16},{20... | collective-permute-start | bytes 786440 | tf_op jit(solution)/shard_map/ppermute | solution.py:17
  188.5 1.0 copy-start.6
Sparse Core Ops, SparseCore 0:
  188.6 44.7 reduce-scatter.1
where the time goes:
time: 245 us; the launch traced here: 242 us
  waiting for transfers between devices  128 us (52%)
  starting transfers between devices  63.7 us (26%)
  matrix products  22.3 us (9%)
  between operations  14.6 us (6%)
  other arithmetic  7.67 us (3%)
  local copies, waits for them, and re-layouts  5.69 us (2%)
    ppermute x14, waiting for transfers between devices, from_behind(): return lax.ppermute(block, axis, route)  85.8 us
    ppermute x14, starting transfers between devices, from_behind(): return lax.ppermute(block, axis, route)  63.7 us
    reduce_scatter x1, waiting for transfers between devices, on_device(): lax.psum_scatter(return_partials(partials).astype(jnp.bfloat16), 'head',...  42 us
  transfers between devices with their start and end apart: 15, of which 15 were waited for; matrix products, arithmetic and copies ran while one was open for 7% of the time, Pallas kernels for 0%

commit v1 on v0

v1 whole, which is shorter than its diff:
```python
import functools
import math

import jax
import jax.numpy as jnp
from jax import lax
from jax.experimental import pallas as pl
from jax.experimental.pallas import tpu as pltpu
from jax.sharding import PartitionSpec as P

MESH = pl.DeviceIdType.MESH
WIN = 8
LINE = 4
NEG = -1e30


def dot_nn(a, b):
    return lax.dot_general(a, b, (((1,), (0,)), ((), ())), preferred_element_type=jnp.float32)


def dot_nt(a, b):
    return lax.dot_general(a, b, (((1,), (1,)), ((), ())), preferred_element_type=jnp.float32)


def kernel(
    shards, docs, len_ref, q_ref, k_ref, v_ref, g_ref,
    att_ref, dq_ref, dk_ref, dv_ref,
    win, p_buf, ds_buf, m_buf, m_now, l_now, acc, delta, begin_buf, qt, gt,
    mine, sib_out, sib_in, out_buf, relay_in, back_in,
    a_send, a_recv, relay_send, fwd_send, fwd_recv, sum_send, sum_recv,
    back_send, back_recv, col_send, col_recv, line_send, line_recv,
):
    me = lax.axis_index("ctx")
    core = lax.axis_index("head")
    tok, width = k_ref.shape
    heads = q_ref.shape[1] // width
    half = tok // 2
    tile = min(256, tok)
    scale = 1.0 / math.sqrt(width)
    scale2 = scale * math.log2(math.e)
    line = me // LINE
    place = me % LINE
    my_rows = pl.ds(pl.multiple_of(core * half, half), half)
    sib_rows = pl.ds(pl.multiple_of((1 - core) * half, half), half)
    sibling = (me, 1 - core)

    def remote(src, dst, send, recv, device):
        return pltpu.make_async_remote_copy(
            src_ref=src, dst_ref=dst, send_sem=send, recv_sem=recv, device_id=device, device_id_type=MESH
        )

    def ahead(step):
        return me + step + LINE * ((place + step) // LINE)

    def behind(step):
        return me - step - LINE * ((LINE - 1 - place + step) // LINE)

    def on_line(step):
        return line * LINE + (place + step + LINE) % LINE

    def distance(slot):
        step = slot % LINE
        wrap = (LINE - 1 - place + step) // LINE
        late = slot // LINE
        return step + LINE * (wrap + late - 2 * wrap * late)

    def exists(slot):
        return me - distance(slot) >= 0

    has_next = me + LINE < shards
    has_prev = line >= 1

    win[0, :, 0:width] = k_ref[...]
    win[0, :, width:] = v_ref[...]

    @pl.when(line < 2)
    def _():
        for slot in range(1, WIN):
            win[slot] = jnp.zeros(win.shape[1:], win.dtype)

    barrier = pltpu.get_barrier_semaphore()

    def greet(device):
        pl.semaphore_signal(barrier, inc=1, device_id=device, device_id_type=MESH)

    greet(sibling)
    for step in range(1, LINE):
        greet((on_line(step), core))
    for step in range(1, LINE):
        up, down = ahead(step), behind(step)
        far_up = jnp.logical_and(place + step >= LINE, up < shards)
        far_down = jnp.logical_and(place < step, down >= 0)

        @pl.when(far_up)
        def _():
            greet((up, core))

        @pl.when(far_down)
        def _():
            greet((down, core))


    @pl.when(has_next)
    def _():
        greet((me + LINE, core))

    @pl.when(has_prev)
    def _():
        greet((me - LINE, core))

    lines = shards // LINE
    near = (line + lines - 1) // lines + 1 - (line + 1) // lines
    far = place * (1 - (line + 2) // lines) + (LINE - 1 - place) * ((line + lines - 2) // lines)
    pl.semaphore_wait(barrier, LINE + near + far)

    def block_send(slot, device):
        return remote(win.at[0, my_rows], win.at[slot, my_rows], a_send.at[slot], a_recv.at[slot], (device, core))

    def relay_copy(step):
        return remote(
            win.at[LINE, my_rows], win.at[LINE + step, my_rows],
            relay_send.at[step], a_recv.at[LINE + step], (on_line(step), core),
        )

    @pl.when(has_next)
    def _():
        block_send(LINE, me + LINE).start()

    for step in range(1, LINE):

        @pl.when(ahead(step) < shards)
        def _():
            block_send(step, ahead(step)).start()

    for h in range(heads):
        qt[:, h * tok : (h + 1) * tok] = q_ref[:, h * width : (h + 1) * width].T
        gt[:, h * tok : (h + 1) * tok] = g_ref[:, h * width : (h + 1) * width].T

    row_pos = me * tok + lax.broadcasted_iota(jnp.int32, (tok, width), 0)
    begin_buf[...] = jnp.zeros((tok, width), jnp.int32)

    def one_doc(doc, first):
        begin_buf[...] = jnp.where(first <= row_pos, first, begin_buf[...])
        return first + len_ref[doc]

    lax.fori_loop(0, docs, one_doc, jnp.int32(0))

    m_now[...] = jnp.full(m_now.shape, NEG, jnp.float32)
    l_now[...] = jnp.zeros(l_now.shape, jnp.float32)
    acc[...] = jnp.zeros(acc.shape, jnp.float32)
    tiles = tok // tile

    def rows_of(index):
        return pl.ds(pl.multiple_of(index * tile, tile), tile)

    def score_pass(slot, own):
        keys = win[slot, :, 0:width]
        vals = win[slot, :, width:]
        key_first = (me - distance(slot)) * tok

        for h in range(heads):

            def body(t, _):
                rows = rows_of(t)
                state = rows_of(t + h * tiles)
                scores = dot_nt(q_ref[rows, h * width : (h + 1) * width], keys) * scale2
                first = begin_buf[rows, 0:1] - key_first
                key_pos = lax.broadcasted_iota(jnp.int32, scores.shape, 1)
                allowed = key_pos >= first
                if own:
                    row = t * tile + lax.broadcasted_iota(jnp.int32, scores.shape, 0)
                    allowed = jnp.logical_and(allowed, key_pos <= row)
                scores = jnp.where(allowed, scores, NEG)
                old = m_now[state, :]
                new = jnp.maximum(old, jnp.max(scores, axis=1, keepdims=True))
                shrink = jnp.exp2(old - new)
                probs = jnp.exp2(scores - new[:, 0:1])
                l_now[state, :] = l_now[state, :] * shrink + jnp.sum(probs, axis=1, keepdims=True)
                m_now[state, :] = new
                m_buf[slot, state, :] = new
                low = probs.astype(jnp.bfloat16)
                p_buf[slot, state, :] = low
                acc[state, :] = acc[state, :] * shrink + dot_nn(low, vals)
                return 0

            lax.fori_loop(0, tiles, body, 0)

    score_pass(0, True)

    def arrival(slot):
        @pl.when(exists(slot))
        def _():
            piece = win.at[slot, my_rows]
            remote(piece, piece, fwd_send.at[slot], a_recv.at[slot], sibling).wait_recv()
            remote(piece, piece, fwd_send.at[slot], fwd_recv.at[slot], sibling).start()

    def arrival_end(slot):
        @pl.when(exists(slot))
        def _():
            piece = win.at[slot, sib_rows]
            remote(piece, piece, fwd_send.at[slot], fwd_recv.at[slot], sibling).wait_recv()

    @pl.when(has_prev)
    def _():
        piece = win.at[LINE, my_rows]
        remote(piece, piece, fwd_send.at[LINE], a_recv.at[LINE], sibling).wait_recv()
        for step in range(1, LINE):
            relay_copy(step).start()
        remote(piece, piece, fwd_send.at[LINE], fwd_recv.at[LINE], sibling).start()

    order = (4, 1, 2, 3, 5, 6, 7)
    for index, slot in enumerate(order):
        if index + 1 < len(order):
            arrival(order[index + 1])
        arrival_end(slot)
        score_pass(slot, False)

    for h in range(heads):

        def finish(t, _):
            rows = rows_of(t)
            state = rows_of(t + h * tiles)
            inverse = 1.0 / l_now[state, :]
            out = (acc[state, :] * inverse).astype(jnp.bfloat16)
            att_ref[rows, h * width : (h + 1) * width] = out
            grads = g_ref[rows, h * width : (h + 1) * width].astype(jnp.float32)
            total = jnp.sum(grads * out.astype(jnp.float32), axis=1, keepdims=True)
            delta[state, :] = jnp.broadcast_to(total, (tile, width))
            l_now[state, :] = inverse
            return 0

        lax.fori_loop(0, tiles, finish, 0)

    def grad_pass(slot):
        vals = win[slot, :, width:]

        for h in range(heads):

            def body(t, _):
                rows = rows_of(t)
                state = rows_of(t + h * tiles)
                factor = jnp.exp2(m_buf[slot, state, :] - m_now[state, :]) * l_now[state, :]
                probs = p_buf[slot, state, :].astype(jnp.float32) * factor[:, 0:1]
                p_buf[slot, state, :] = probs.astype(jnp.bfloat16)
                prob_grad = dot_nt(g_ref[rows, h * width : (h + 1) * width], vals)
                ds_buf[slot, state, :] = (probs * (prob_grad - delta[state, 0:1])).astype(jnp.bfloat16)
                return 0

            lax.fori_loop(0, tiles, body, 0)
        for top, left, right in ((0, qt, ds_buf), (width, gt, p_buf)):
            part = dot_nn(left[...], right[slot])
            bottom = top + width

            @pl.when(core == 0)
            def _():
                mine[slot, top:bottom, :] = part[:, 0:half]
                sib_out[slot, top:bottom, :] = part[:, half:].astype(jnp.bfloat16)

            @pl.when(core == 1)
            def _():
                mine[slot, top:bottom, :] = part[:, half:]
                sib_out[slot, top:bottom, :] = part[:, 0:half].astype(jnp.bfloat16)

    def sum_copy(slot):
        return remote(sib_out.at[slot], sib_in.at[slot], sum_send.at[slot], sum_recv.at[slot], sibling)

    def back_copy(step):
        return remote(
            out_buf.at[step], back_in.at[step], back_send.at[step], back_recv.at[step], (behind(step), core)
        )

    def line_copy(step):
        return remote(
            out_buf.at[LINE + step], relay_in.at[step], line_send.at[step], line_recv.at[step], (on_line(-step), core)
        )

    def col_copy():
        return remote(out_buf.at[LINE], back_in.at[0], col_send.at[0], col_recv.at[0], (me - LINE, core))

    def return_part(slot):
        sum_copy(slot).wait_recv()
        total = mine[slot] + sib_in[slot].astype(jnp.float32)
        mine[slot] = total
        out_buf[slot] = total.astype(jnp.bfloat16)

        if slot > LINE:

            @pl.when(has_prev)
            def _():
                line_copy(slot - LINE).start()

        if 0 < slot < LINE:

            @pl.when(exists(slot))
            def _():
                back_copy(slot).start()

    back_order = (5, 6, 7, 4, 1, 2, 3, 0)
    for index, slot in enumerate(back_order):
        grad_pass(slot)
        sum_copy(slot).start()
        if index > 0:
            return_part(back_order[index - 1])
    return_part(back_order[-1])

    @pl.when(has_prev)
    def _():
        for step in range(1, LINE):
            line_copy(step).wait_recv()
        total = mine[LINE]
        for step in range(1, LINE):
            total = total + relay_in[step].astype(jnp.float32)
        out_buf[LINE] = total.astype(jnp.bfloat16)
        col_copy().start()

    for h in range(heads):

        def query_tile(t, _):
            rows = rows_of(t)
            state = rows_of(t + h * tiles)
            total = jnp.zeros((tile, width), jnp.float32)
            for slot in range(WIN):
                total = total + dot_nn(ds_buf[slot, state, :], win[slot, :, 0:width])
            dq_ref[rows, h * width : (h + 1) * width] = (total * scale).astype(jnp.bfloat16)
            return 0

        lax.fori_loop(0, tiles, query_tile, 0)

    for step in range(1, LINE):

        @pl.when(ahead(step) < shards)
        def _():
            back_copy(step).wait_recv()
            mine[0] = mine[0] + back_in[step].astype(jnp.float32)

    @pl.when(has_next)
    def _():
        col_copy().wait_recv()
        mine[0] = mine[0] + back_in[0].astype(jnp.float32)

    dk_ref[...] = (mine[0, 0:width, :] * scale).T.astype(jnp.bfloat16)
    dv_ref[...] = mine[0, width:, :].T.astype(jnp.bfloat16)

    @pl.when(has_next)
    def _():
        block_send(LINE, me + LINE).wait_send()

    for step in range(1, LINE):

        @pl.when(ahead(step) < shards)
        def _():
            block_send(step, ahead(step)).wait_send()

    @pl.when(has_prev)
    def _():
        for step in range(1, LINE):
            relay_copy(step).wait_send()
            line_copy(step).wait_send()
        col_copy().wait_send()

    for slot in range(1, WIN):

        @pl.when(exists(slot))
        def _():
            piece = win.at[slot, my_rows]
            remote(piece, piece, fwd_send.at[slot], fwd_recv.at[slot], sibling).wait_send()

    for slot in range(WIN):
        sum_copy(slot).wait_send()

    for step in range(1, LINE):

        @pl.when(behind(step) >= 0)
        def _():
            back_copy(step).wait_send()


def solution(mesh):
    shards = mesh.shape["ctx"]

    def on_device(queries, keys, values, out_grad, lengths):
        tok, width = keys.shape
        heads = queries.shape[1] // width
        rows = heads * tok
        half = tok // 2
        bf16, f32 = jnp.bfloat16, jnp.float32
        vmem = pl.BlockSpec(memory_space=pltpu.VMEM)
        dma = pltpu.SemaphoreType.DMA
        flops = 6 * 2 * rows * WIN * tok * width
        return pl.pallas_call(
            functools.partial(kernel, shards, lengths.shape[0]),
            out_shape=(
                jax.ShapeDtypeStruct(queries.shape, bf16),
                jax.ShapeDtypeStruct(queries.shape, bf16),
                jax.ShapeDtypeStruct((half, width), bf16),
                jax.ShapeDtypeStruct((half, width), bf16),
            ),
            in_specs=[pl.BlockSpec(memory_space=pltpu.SMEM)] + [vmem] * 4,
            out_specs=(vmem,) * 4,
            scratch_shapes=[
                pltpu.VMEM((WIN, tok, 2 * width), bf16),
                pltpu.VMEM((WIN, rows, tok), bf16),
                pltpu.VMEM((WIN, rows, tok), bf16),
                pltpu.VMEM((WIN, rows, width), f32),
                pltpu.VMEM((rows, width), f32),
                pltpu.VMEM((rows, width), f32),
                pltpu.VMEM((rows, width), f32),
                pltpu.VMEM((rows, width), f32),
                pltpu.VMEM((tok, width), jnp.int32),
                pltpu.VMEM((width, rows), bf16),
                pltpu.VMEM((width, rows), bf16),
                pltpu.VMEM((WIN, 2 * width, half), f32),
                pltpu.VMEM((WIN, 2 * width, half), bf16),
                pltpu.VMEM((WIN, 2 * width, half), bf16),
                pltpu.VMEM((WIN, 2 * width, half), bf16),
                pltpu.VMEM((LINE, 2 * width, half), bf16),
                pltpu.VMEM((LINE, 2 * width, half), bf16),
                dma((WIN,)), dma((WIN,)), dma((LINE,)), dma((WIN,)), dma((WIN,)), dma((WIN,)), dma((WIN,)),
                dma((LINE,)), dma((LINE,)), dma((1,)), dma((1,)), dma((LINE,)), dma((LINE,)),
            ],
            compiler_params=pltpu.CompilerParams(
                collective_id=0, has_side_effects=True, vmem_limit_bytes=56 * 1024 * 1024
            ),
            cost_estimate=pl.CostEstimate(flops=flops, bytes_accessed=1 << 21, transcendentals=rows * WIN * tok),
            name="packed_attention",
        )(lengths, queries, keys, values, out_grad)

    return jax.shard_map(
        on_device,
        mesh=mesh,
        in_specs=(P("ctx", "head"), P("ctx", None), P("ctx", None), P("ctx", "head"), P()),
        out_specs=(P("ctx", "head"), P("ctx", "head"), P(("ctx", "head"), None), P(("ctx", "head"), None)),
        check_vma=False,
    )
```

time: 245 us -> 72.2 us (0.29); the launches traced: 242 us -> 72 us
  waiting for transfers between devices: 128 us -> 0 us
  Pallas kernels: 0 us -> 67.2 us
  starting transfers between devices: 63.7 us -> 0 us
  matrix products: 22.3 us -> 0 us
  between operations: 14.6 us -> 0.65 us
  other arithmetic: 7.67 us -> 0 us
    ppermute x14 -> x0, waiting for transfers between devices: 85.8 us -> none  [from_behind(): return lax.ppermute(block, axis, route)]
    pallas_call x0 -> x1, Pallas kernels: none -> 67.2 us  [on_device(): pl.pallas_call(functools.partial(kernel, shards, lengths.shape[0]), out_s...]
    ppermute x14 -> x0, starting transfers between devices: 63.7 us -> none  [from_behind(): return lax.ppermute(block, axis, route)]
    reduce_scatter x1 -> x0, waiting for transfers between devices: 42 us -> none  [on_device(): lax.psum_scatter(return_partials(partials).astype(jnp.bfloat16), 'head',...]
    dot_general x48 -> x0, matrix products: 22.3 us -> none  [the longest x8 4.43 us: masked_scores(): jnp.einsum('rhd,cd->hrc', query_heads, block_keys, preferred_element_type...]
  transfers between devices with their start and end apart: 15 -> 0, of which waited for: 15 -> 0; matrix products, arithmetic and copies ran while one was open for 7% -> 0% of each run, Pallas kernels for 0% -> 0%
where the time goes in v1:
time: 72.2 us; the launch traced here: 72 us
  Pallas kernels  67.2 us (93%)
  local copies, waits for them, and re-layouts  4.07 us (6%)
    pallas_call x1, Pallas kernels, on_device(): pl.pallas_call(functools.partial(kernel, shards, lengths.shape[0]), out_s...  67.2 us
    unnamed x10, local copies, waits for them, and re-layouts  4.07 us

profile of v1, /device:TPU:97, one launch (start us, length us, event | category | flops | bytes accessed | tf_op | source)
XLA Modules:
  0.0 72.0 jit_solution(4984619054704496843)
XLA Ops:
  0.6 67.2 %packed_attention.1 = (bf16[512,256]{1,0:T(8,128)(2,1)}, bf16[512,256]{1,0:T(8,128)(2,1)}, bf16[256,128]{1,0:T(8,128)(2,1)}, bf16[256,128]{1,0:T(8,128)(2,1)}) custom-call(s32[64]{0:T(128)} %len_ref.1, bf16[512,256]{1,0:T(8,128)(2,1)} %q_ref.1, bf16[512,128]{1,0:T(8,128)(2,1)} %k_ref.1, bf16[512,128]{1,0:T(8,128)(2,1)} %v_ref.1, bf16[512,256]{1,0:T(8,128)(2,1)} %g_ref.1), custom_call_target="tpu_custom_call" | custom-call | flops 6442450944 | bytes 2097152 | tf_op jit(solution)/shard_map/packed_attention/pallas_call | solution.py:390
  67.9 0.0 copy-start
  67.9 1.7 %copy.13 = bf16[512,256]{1,0:T(8,128)(2,1)} copy(bf16[512,256]{1,0:T(8,128)(2,1)} %get-tuple-element.8) | data formatting | bytes 524288
  69.6 0.0 copy-done
  69.6 0.0 copy-start.2
  69.6 0.7 copy.14
  70.3 0.2 copy-done.2
  70.5 0.0 copy-start.1
  70.5 0.6 copy.15
  71.1 0.2 copy-done.1
  71.3 0.6 copy.16
Async XLA Ops:
  67.9 1.7 %copy-start = (bf16[512,256]{1,0:T(8,128)(2,1)S(1)}, bf16[512,256]{1,0:T(8,128)(2,1)}, u32[]{:S(2)}) copy-start(bf16[512,256]{1,0:T(8,128)(2,1)} %get-tuple-element.9) | copy-start | bytes 786436
  69.6 0.9 %copy-start.2 = (bf16[256,128]{1,0:T(8,128)(2,1)S(1)}, bf16[256,128]{1,0:T(8,128)(2,1)}, u32[]{:S(2)}) copy-start(bf16[256,128]{1,0:T(8,128)(2,1)} %get-tuple-element.10) | copy-start | bytes 196612
  70.5 0.9 %copy-start.1 = (bf16[256,128]{1,0:T(8,128)(2,1)S(1)}, bf16[256,128]{1,0:T(8,128)(2,1)}, u32[]{:S(2)}) copy-start(bf16[256,128]{1,0:T(8,128)(2,1)} %get-tuple-element.11) | copy-start | bytes 196612

commit v2 on v1

v2 whole, which is shorter than its diff:
```python
import functools
import math

import jax
import jax.numpy as jnp
from jax import lax
from jax.experimental import pallas as pl
from jax.experimental.pallas import tpu as pltpu
from jax.sharding import PartitionSpec as P

MESH = pl.DeviceIdType.MESH
WIN = 8
LINE = 4
CHUNKS = 2
NEG = -1e30


def dot_nn(a, b):
    return lax.dot_general(a, b, (((1,), (0,)), ((), ())), preferred_element_type=jnp.float32)


def dot_nt(a, b):
    return lax.dot_general(a, b, (((1,), (1,)), ((), ())), preferred_element_type=jnp.float32)


def kernel(
    shards, docs, len_ref, q_hbm, k_hbm, v_hbm, g_hbm,
    att_ref, dq_ref, dk_ref, dv_ref,
    fetch_sem, q_ref, g_ref, win, p_buf, ds_buf, s_buf, m_buf, m_now, l_now, acc, q_ext, g_ext, qt, gt,
    kept, mine, sib_out, sib_in, out_buf, relay_in, back_in,
    a_send, a_recv, relay_send, fwd_send, fwd_recv, sum_send, sum_recv,
    back_send, back_recv, col_send, col_recv, line_send, line_recv,
):
    me = lax.axis_index("ctx")
    core = lax.axis_index("head")
    tok, width = k_hbm.shape
    heads = q_hbm.shape[1] // width
    half = tok // 2
    scale = 1.0 / math.sqrt(width)
    scale2 = scale * math.log2(math.e)
    line = me // LINE
    place = me % LINE
    my_rows = pl.ds(pl.multiple_of(core * half, half), half)
    sib_rows = pl.ds(pl.multiple_of((1 - core) * half, half), half)
    quarter = half // CHUNKS

    def chunk_rows(whose, chunk):
        return pl.ds(pl.multiple_of(whose * half + chunk * quarter, quarter), quarter)
    sibling = (me, 1 - core)

    def remote(src, dst, send, recv, device):
        return pltpu.make_async_remote_copy(
            src_ref=src, dst_ref=dst, send_sem=send, recv_sem=recv, device_id=device, device_id_type=MESH
        )

    def ahead(step):
        return me + step + LINE * ((place + step) // LINE)

    def behind(step):
        return me - step - LINE * ((LINE - 1 - place + step) // LINE)

    def on_line(step):
        return line * LINE + (place + step + LINE) % LINE

    def distance(slot):
        step = slot % LINE
        wrap = (LINE - 1 - place + step) // LINE
        late = slot // LINE
        return step + LINE * (wrap + late - 2 * wrap * late)

    def exists(slot):
        return me - distance(slot) >= 0

    has_next = me + LINE < shards
    has_prev = line >= 1

    fetches = [
        pltpu.make_async_copy(source, target, fetch_sem.at[index])
        for index, (source, target) in enumerate(
            (
                (k_hbm, win.at[0, :, pl.ds(0, width)]),
                (v_hbm, win.at[0, :, pl.ds(width, width)]),
                (q_hbm, q_ref),
                (g_hbm, g_ref),
            )
        )
    ]
    for fetch in fetches:
        fetch.start()

    @pl.when(line < 2)
    def _():
        for slot in range(1, WIN):
            win[slot] = jnp.zeros(win.shape[1:], win.dtype)

    barrier = pltpu.get_barrier_semaphore()

    def greet(device):
        pl.semaphore_signal(barrier, inc=1, device_id=device, device_id_type=MESH)

    greet(sibling)
    for step in range(1, LINE):
        greet((on_line(step), core))
    for step in range(1, LINE):
        up, down = ahead(step), behind(step)
        far_up = jnp.logical_and(place + step >= LINE, up < shards)
        far_down = jnp.logical_and(place < step, down >= 0)

        @pl.when(far_up)
        def _():
            greet((up, core))

        @pl.when(far_down)
        def _():
            greet((down, core))


    @pl.when(has_next)
    def _():
        greet((me + LINE, core))

    @pl.when(has_prev)
    def _():
        greet((me - LINE, core))

    lines = shards // LINE
    near = (line + lines - 1) // lines + 1 - (line + 1) // lines
    far = place * (1 - (line + 2) // lines) + (LINE - 1 - place) * ((line + lines - 2) // lines)
    pl.semaphore_wait(barrier, LINE + near + far)
    fetches[0].wait()
    fetches[1].wait()

    def block_send(slot, device, chunk):
        rows = chunk_rows(core, chunk)
        return remote(
            win.at[0, rows], win.at[slot, rows], a_send.at[slot, chunk], a_recv.at[slot, chunk], (device, core)
        )

    def relay_copy(step, chunk):
        rows = chunk_rows(core, chunk)
        return remote(
            win.at[LINE, rows], win.at[LINE + step, rows],
            relay_send.at[step, chunk], a_recv.at[LINE + step, chunk], (on_line(step), core),
        )

    @pl.when(has_next)
    def _():
        for chunk in range(CHUNKS):
            block_send(LINE, me + LINE, chunk).start()

    for step in range(1, LINE):

        @pl.when(ahead(step) < shards)
        def _():
            for chunk in range(CHUNKS):
                block_send(step, ahead(step), chunk).start()

    lane = lax.broadcasted_iota(jnp.int32, (tok, width), 1)
    sub = lax.broadcasted_iota(jnp.int32, (tok, width), 0)

    def one_doc(doc, state):
        first, starts, ends = state
        here = lane[0:8] == doc
        last = first + len_ref[doc]
        return last, jnp.where(here, first, starts), jnp.where(here, last, ends)

    zero = jnp.zeros((8, width), jnp.int32)
    _, starts, ends = lax.fori_loop(0, docs, one_doc, (jnp.int32(0), zero, zero))
    starts, ends = starts[0:1], ends[0:1]
    row_pos = me * tok + sub
    inside = jnp.logical_and(row_pos >= starts, row_pos < ends)
    marks = jnp.where(inside, NEG, 0.0).astype(jnp.bfloat16)
    fetches[2].wait()
    fetches[3].wait()
    for h in range(heads):
        q_ext[h, :, 0:width] = q_ref[:, h * width : (h + 1) * width]
        q_ext[h, :, width:] = marks
    acc[...] = jnp.zeros(acc.shape, jnp.float32)
    m_now[...] = jnp.full(m_now.shape, NEG, jnp.float32)
    ones = jnp.ones((tok, width), jnp.bfloat16)

    def wide(x):
        return jnp.concatenate([x] * (tok // width), axis=1)

    def score_pass(slot, own):
        early = ((me - distance(slot)) * tok + sub) < starts
        keys = jnp.concatenate([win[slot, :, 0:width], early.astype(jnp.bfloat16)], axis=1)
        vals = jnp.concatenate([win[slot, :, width:], ones], axis=1)
        for h in range(heads):
            rows = slice(h * tok, (h + 1) * tok)
            scores = dot_nt(q_ext[h], keys)
            if own:
                col = lax.broadcasted_iota(jnp.int32, scores.shape, 1)
                row = lax.broadcasted_iota(jnp.int32, scores.shape, 0)
                scores = jnp.where(col <= row, scores, NEG)
            s_buf[h] = scores
            peak = jnp.max(scores, axis=1, keepdims=True) * scale2
            m_buf[slot, rows, :] = jnp.maximum(m_now[rows, :], peak)
        for h in range(heads):
            rows = slice(h * tok, (h + 1) * tok)
            new = m_buf[slot, rows, :]
            shrink = jnp.exp2(m_now[rows, :] - new)
            m_now[rows, :] = new
            low = jnp.exp2(s_buf[h] * scale2 - wide(new)).astype(jnp.bfloat16)
            p_buf[slot, rows, :] = low
            part = dot_nn(low, vals)
            acc[rows, 0:width] = acc[rows, 0:width] * shrink + part[:, 0:width]
            acc[rows, width:] = acc[rows, width:] * shrink + part[:, width:]

    score_pass(0, True)
    for h in range(heads):
        qt[:, h * tok : (h + 1) * tok] = q_ref[:, h * width : (h + 1) * width].T
        gt[:, h * tok : (h + 1) * tok] = g_ref[:, h * width : (h + 1) * width].T

    def cross_copy(slot, chunk):
        piece = win.at[slot, chunk_rows(core, chunk)]
        return remote(piece, piece, fwd_send.at[slot, chunk], fwd_recv.at[slot, chunk], sibling)

    def arrival(slot):
        @pl.when(exists(slot))
        def _():
            for chunk in range(CHUNKS):
                piece = win.at[slot, chunk_rows(core, chunk)]
                remote(piece, piece, fwd_send.at[slot, chunk], a_recv.at[slot, chunk], sibling).wait_recv()
                if slot == LINE:
                    for step in range(1, LINE):
                        relay_copy(step, chunk).start()
                cross_copy(slot, chunk).start()

    def arrival_end(slot):
        @pl.when(exists(slot))
        def _():
            for chunk in range(CHUNKS):
                piece = win.at[slot, chunk_rows(1 - core, chunk)]
                remote(piece, piece, fwd_send.at[slot, chunk], fwd_recv.at[slot, chunk], sibling).wait_recv()

    arrival(LINE)
    order = (4, 1, 2, 3, 5, 6, 7)
    for index, slot in enumerate(order):
        if index + 1 < len(order):
            arrival(order[index + 1])
        arrival_end(slot)
        score_pass(slot, False)

    for h in range(heads):
        rows = slice(h * tok, (h + 1) * tok)
        cols = slice(h * width, (h + 1) * width)
        inverse = 1.0 / acc[rows, width:]
        out = (acc[rows, 0:width] * inverse).astype(jnp.bfloat16)
        att_ref[:, cols] = out
        grads = g_ref[:, cols]
        total = -jnp.sum(grads.astype(jnp.float32) * out.astype(jnp.float32), axis=1, keepdims=True)
        high = total.astype(jnp.bfloat16).astype(jnp.float32)
        extra = jnp.where(lane == 0, high, jnp.where(lane == 1, total - high, 0.0))
        g_ext[h, :, 0:width] = grads
        g_ext[h, :, width:] = extra.astype(jnp.bfloat16)
        l_now[rows, :] = inverse

    def factor_pass(slot):
        vals = jnp.concatenate([win[slot, :, width:], ones], axis=1)
        for h in range(heads):
            rows = slice(h * tok, (h + 1) * tok)
            factor = jnp.exp2(m_buf[slot, rows, :] - m_now[rows, :]) * l_now[rows, :]
            probs = p_buf[slot, rows, :].astype(jnp.float32) * wide(factor)
            prob_grad = dot_nt(g_ext[h], vals)
            ds_buf[slot, rows, :] = (probs * prob_grad).astype(jnp.bfloat16)
            p_buf[slot, rows, :] = probs.astype(jnp.bfloat16)

    halves = (0, 1)

    def part_rows(part):
        return pl.ds(part * width, width)

    def sum_copy(slot, part):
        rows = part_rows(part)
        return remote(
            sib_out.at[slot, rows, sib_rows], sib_in.at[slot, rows], sum_send.at[slot, part], sum_recv.at[slot, part], sibling
        )

    def back_copy(step):
        return remote(
            out_buf.at[step], back_in.at[step], back_send.at[step], back_recv.at[step], (behind(step), core)
        )

    def line_copy(step, part):
        rows = part_rows(part)
        return remote(
            out_buf.at[LINE + step, rows], relay_in.at[step, rows],
            line_send.at[step, part], line_recv.at[step, part], (on_line(-step), core),
        )

    def col_copy(part):
        rows = part_rows(part)
        return remote(
            out_buf.at[LINE, rows], back_in.at[0, rows], col_send.at[part], col_recv.at[part], (me - LINE, core)
        )

    sides = ((1, gt, p_buf), (0, qt, ds_buf))

    def grad_pass(slot):
        for part, left, right in sides:
            total = dot_nn(left[...], right[slot])
            mine[slot, part_rows(part), :] = total
            sib_out[slot, part_rows(part), :] = total.astype(jnp.bfloat16)
            sum_copy(slot, part).start()

    def return_part(slot):
        for part, _, _ in sides:
            rows = part_rows(part)
            sum_copy(slot, part).wait_recv()
            total = mine[slot, rows, my_rows] + sib_in[slot, rows, :].astype(jnp.float32)
            if slot in (0, LINE):
                kept[slot // LINE, rows, :] = total
            else:
                out_buf[slot, rows, :] = total.astype(jnp.bfloat16)
            if slot > LINE:

                @pl.when(has_prev)
                def _():
                    line_copy(slot - LINE, part).start()

        if 0 < slot < LINE:

            @pl.when(exists(slot))
            def _():
                back_copy(slot).start()

    back_order = (6, 5, 7, 3, 2, 1, 4, 0)
    for index in range(WIN + 2):
        if 1 <= index <= WIN:
            grad_pass(back_order[index - 1])
        if index < WIN:
            factor_pass(back_order[index])
        if index >= 2:
            return_part(back_order[index - 2])

    @pl.when(has_prev)
    def _():
        for part, _, _ in sides:
            rows = part_rows(part)
            total = kept[1, rows, :]
            for step in range(1, LINE):
                line_copy(step, part).wait_recv()
                total = total + relay_in[step, rows, :].astype(jnp.float32)
            out_buf[LINE, rows, :] = total.astype(jnp.bfloat16)
            col_copy(part).start()

    for h in range(heads):
        rows = slice(h * tok, (h + 1) * tok)
        total = dot_nn(ds_buf[0, rows, :], win[0, :, 0:width])
        for slot in range(1, WIN):
            total = total + dot_nn(ds_buf[slot, rows, :], win[slot, :, 0:width])
        dq_ref[:, h * width : (h + 1) * width] = (total * scale).astype(jnp.bfloat16)

    for step in range(1, LINE):

        @pl.when(ahead(step) < shards)
        def _():
            back_copy(step).wait_recv()
            kept[0] = kept[0] + back_in[step].astype(jnp.float32)

    for part, _, _ in sides:
        rows = part_rows(part)

        @pl.when(has_next)
        def _():
            col_copy(part).wait_recv()
            kept[0, rows, :] = kept[0, rows, :] + back_in[0, rows, :].astype(jnp.float32)

        if part:
            dv_ref[...] = kept[0, rows, :].T.astype(jnp.bfloat16)
        else:
            dk_ref[...] = (kept[0, rows, :] * scale).T.astype(jnp.bfloat16)

    @pl.when(has_next)
    def _():
        for chunk in range(CHUNKS):
            block_send(LINE, me + LINE, chunk).wait_send()

    for step in range(1, LINE):

        @pl.when(ahead(step) < shards)
        def _():
            for chunk in range(CHUNKS):
                block_send(step, ahead(step), chunk).wait_send()

    @pl.when(has_prev)
    def _():
        for step in range(1, LINE):
            for chunk in range(CHUNKS):
                relay_copy(step, chunk).wait_send()
            for part in halves:
                line_copy(step, part).wait_send()
        for part in halves:
            col_copy(part).wait_send()

    for slot in range(1, WIN):

        @pl.when(exists(slot))
        def _():
            for chunk in range(CHUNKS):
                cross_copy(slot, chunk).wait_send()

    for slot in range(WIN):
        for part in halves:
            sum_copy(slot, part).wait_send()

    for step in range(1, LINE):

        @pl.when(behind(step) >= 0)
        def _():
            back_copy(step).wait_send()


def hand_on(*refs):
    for source, target in zip(refs[:4], refs[4:]):
        target[...] = source[...]


def solution(mesh):
    shards = mesh.shape["ctx"]

    def on_device(queries, keys, values, out_grad, lengths):
        tok, width = keys.shape
        heads = queries.shape[1] // width
        rows = heads * tok
        half = tok // 2
        bf16, f32 = jnp.bfloat16, jnp.float32
        vmem = pl.BlockSpec(memory_space=pltpu.VMEM)
        dma = pltpu.SemaphoreType.DMA
        flops = 6 * 2 * rows * WIN * tok * width
        results = pl.pallas_call(
            functools.partial(kernel, shards, lengths.shape[0]),
            out_shape=(
                jax.ShapeDtypeStruct(queries.shape, bf16),
                jax.ShapeDtypeStruct(queries.shape, bf16),
                jax.ShapeDtypeStruct((half, width), bf16),
                jax.ShapeDtypeStruct((half, width), bf16),
            ),
            in_specs=[pl.BlockSpec(memory_space=pltpu.SMEM)] + [pl.BlockSpec(memory_space=pl.ANY)] * 4,
            out_specs=(vmem,) * 4,
            scratch_shapes=[
                dma((4,)),
                pltpu.VMEM(queries.shape, bf16),
                pltpu.VMEM(queries.shape, bf16),
                pltpu.VMEM((WIN, tok, 2 * width), bf16),
                pltpu.VMEM((WIN, rows, tok), bf16),
                pltpu.VMEM((WIN, rows, tok), bf16),
                pltpu.VMEM((heads, tok, tok), f32),
                pltpu.VMEM((WIN, rows, width), f32),
                pltpu.VMEM((rows, width), f32),
                pltpu.VMEM((rows, width), f32),
                pltpu.VMEM((rows, 2 * width), f32),
                pltpu.VMEM((heads, tok, 2 * width), bf16),
                pltpu.VMEM((heads, tok, 2 * width), bf16),
                pltpu.VMEM((width, rows), bf16),
                pltpu.VMEM((width, rows), bf16),
                pltpu.VMEM((2, 2 * width, half), f32),
                pltpu.VMEM((WIN, 2 * width, tok), f32),
                pltpu.VMEM((WIN, 2 * width, tok), bf16),
                pltpu.VMEM((WIN, 2 * width, half), bf16),
                pltpu.VMEM((WIN, 2 * width, half), bf16),
                pltpu.VMEM((LINE, 2 * width, half), bf16),
                pltpu.VMEM((LINE, 2 * width, half), bf16),
                dma((WIN, CHUNKS)), dma((WIN, CHUNKS)), dma((LINE, CHUNKS)), dma((WIN, CHUNKS)), dma((WIN, CHUNKS)),
                dma((WIN, 2)), dma((WIN, 2)), dma((LINE,)), dma((LINE,)), dma((2,)), dma((2,)),
                dma((LINE, 2)), dma((LINE, 2)),
            ],
            compiler_params=pltpu.CompilerParams(
                collective_id=0, has_side_effects=True, vmem_limit_bytes=56 * 1024 * 1024
            ),
            cost_estimate=pl.CostEstimate(flops=flops, bytes_accessed=1 << 21, transcendentals=rows * WIN * tok),
            name="packed_attention",
        )(lengths, queries, keys, values, out_grad)
        return pl.pallas_call(
            hand_on,
            out_shape=tuple(jax.ShapeDtypeStruct(r.shape, r.dtype) for r in results),
            in_specs=[vmem] * 4,
            out_specs=(vmem,) * 4,
            name="hand_on",
        )(*results)

    return jax.shard_map(
        on_device,
        mesh=mesh,
        in_specs=(P("ctx", "head"), P("ctx", None), P("ctx", None), P("ctx", "head"), P()),
        out_specs=(P("ctx", "head"), P("ctx", "head"), P(("ctx", "head"), None), P(("ctx", "head"), None)),
        check_vma=False,
    )
```

time: 72.2 us -> 53.2 us (0.74)
  Pallas kernels: 67.2 us -> 52.4 us
  local copies, waits for them, and re-layouts: 4.07 us -> 0 us
    pallas_call x1, Pallas kernels: 67.2 us -> 50.6 us  [on_device(): pl.pallas_call(functools.partial(kernel, shards, lengths.shape[0]), out_s...]
    unnamed x10 -> x0, local copies, waits for them, and re-layouts: 4.07 us -> none
    pallas_call x0 -> x1, Pallas kernels: none -> 1.88 us  [on_device(): pl.pallas_call(hand_on, out_shape=tuple((jax.ShapeDtypeStruct(r.shape, r....]
where the time goes in v2:
time: 53.2 us; the launch traced here: 53.1 us
  Pallas kernels  52.4 us (98%)
  between operations  0.64 us (1%)
    pallas_call x1, Pallas kernels, on_device(): pl.pallas_call(functools.partial(kernel, shards, lengths.shape[0]), out_s...  50.6 us
    pallas_call x1, Pallas kernels, on_device(): pl.pallas_call(hand_on, out_shape=tuple((jax.ShapeDtypeStruct(r.shape, r....  1.88 us

profile of v2, /device:TPU:97, one launch (start us, length us, event | category | flops | bytes accessed | tf_op | source)
XLA Modules:
  0.0 53.1 jit_solution(10176067158372676239)
XLA Ops:
  0.6 50.6 %packed_attention.1 = (bf16[512,256]{1,0:T(8,128)(2,1)}, bf16[512,256]{1,0:T(8,128)(2,1)}, bf16[256,128]{1,0:T(8,128)(2,1)}, bf16[256,128]{1,0:T(8,128)(2,1)}) custom-call(s32[64]{0:T(128)} %len_ref.1, bf16[512,256]{1,0:T(8,128)(2,1)} %q_hbm.1, bf16[512,128]{1,0:T(8,128)(2,1)} %k_hbm.1, bf16[512,128]{1,0:T(8,128)(2,1)} %v_hbm.1, bf16[512,256]{1,0:T(8,128)(2,1)} %g_hbm.1), custom_call_target="tpu_custom_call" | custom-call | flops 6442450944 | bytes 2097152 | tf_op jit(solution)/shard_map/packed_attention/pallas_call | solution.py:432
  51.2 1.9 %hand_on.1 = (bf16[512,256]{1,0:T(8,128)(2,1)}, bf16[512,256]{1,0:T(8,128)(2,1)}, bf16[256,128]{1,0:T(8,128)(2,1)}, bf16[256,128]{1,0:T(8,128)(2,1)}) custom-call(bf16[512,256]{1,0:T(8,128)(2,1)} %get-tuple-element.8.refs_0_, bf16[512,256]{1,0:T(8,128)(2,1)} %get-tuple-element.9.refs_1_, bf16[256,128]{1,0:T(8,128)(2,1)} %get-tuple-element.10.refs_2_, ...), custom_call_target="tpu_custom_call" | custom-call | tf_op jit(solution)/shard_map/hand_on/pallas_call | solution.py:475

commit v3 on v2

--- a/solution.py
+++ b/solution.py
@@ -249,7 +249,10 @@
         out = (acc[rows, 0:width] * inverse).astype(jnp.bfloat16)
         att_ref[:, cols] = out
         grads = g_ref[:, cols]
-        total = -jnp.sum(grads.astype(jnp.float32) * out.astype(jnp.float32), axis=1, keepdims=True)
+        terms = grads.astype(jnp.float32) * out.astype(jnp.float32)
+        coarse = terms.astype(jnp.bfloat16)
+        fine = (terms - coarse.astype(jnp.float32)).astype(jnp.bfloat16)
+        total = -dot_nn(jnp.concatenate([coarse, fine], axis=1), jnp.ones((2 * width, width), jnp.bfloat16))
         high = total.astype(jnp.bfloat16).astype(jnp.float32)
         extra = jnp.where(lane == 0, high, jnp.where(lane == 1, total - high, 0.0))
         g_ext[h, :, 0:width] = grads
@@ -329,10 +332,10 @@
     for index in range(WIN + 2):
         if 1 <= index <= WIN:
             grad_pass(back_order[index - 1])
+        if index >= 2:
+            return_part(back_order[index - 2])
         if index < WIN:
             factor_pass(back_order[index])
-        if index >= 2:
-            return_part(back_order[index - 2])
 
     @pl.when(has_prev)
     def _():

time: 53.2 us -> 52.3 us (0.983)
  Pallas kernels: 52.4 us -> 51.6 us
    pallas_call x1, Pallas kernels: 50.6 us -> 49.7 us  [on_device(): pl.pallas_call(functools.partial(kernel, shards, lengths.shape[0]), out_s...]
where the time goes in v3:
time: 52.3 us; the launch traced here: 52.2 us
  Pallas kernels  51.6 us (99%)
  between operations  0.64 us (1%)
    pallas_call x1, Pallas kernels, on_device(): pl.pallas_call(functools.partial(kernel, shards, lengths.shape[0]), out_s...  49.7 us
    pallas_call x1, Pallas kernels, on_device(): pl.pallas_call(hand_on, out_shape=tuple((jax.ShapeDtypeStruct(r.shape, r....  1.88 us

profile of v3, /device:TPU:97, one launch (start us, length us, event | category | flops | bytes accessed | tf_op | source)
XLA Modules:
  0.0 52.2 jit_solution(6865605084476146193)
XLA Ops:
  0.6 49.7 %packed_attention.1 = (bf16[512,256]{1,0:T(8,128)(2,1)}, bf16[512,256]{1,0:T(8,128)(2,1)}, bf16[256,128]{1,0:T(8,128)(2,1)}, bf16[256,128]{1,0:T(8,128)(2,1)}) custom-call(s32[64]{0:T(128)} %len_ref.1, bf16[512,256]{1,0:T(8,128)(2,1)} %q_hbm.1, bf16[512,128]{1,0:T(8,128)(2,1)} %k_hbm.1, bf16[512,128]{1,0:T(8,128)(2,1)} %v_hbm.1, bf16[512,256]{1,0:T(8,128)(2,1)} %g_hbm.1), custom_call_target="tpu_custom_call" | custom-call | flops 6442450944 | bytes 2097152 | tf_op jit(solution)/shard_map/packed_attention/pallas_call | solution.py:435
  50.3 1.9 %hand_on.1 = (bf16[512,256]{1,0:T(8,128)(2,1)}, bf16[512,256]{1,0:T(8,128)(2,1)}, bf16[256,128]{1,0:T(8,128)(2,1)}, bf16[256,128]{1,0:T(8,128)(2,1)}) custom-call(bf16[512,256]{1,0:T(8,128)(2,1)} %get-tuple-element.8.refs_0_, bf16[512,256]{1,0:T(8,128)(2,1)} %get-tuple-element.9.refs_1_, bf16[256,128]{1,0:T(8,128)(2,1)} %get-tuple-element.10.refs_2_, ...), custom_call_target="tpu_custom_call" | custom-call | tf_op jit(solution)/shard_map/hand_on/pallas_call | solution.py:478

commit v4 on v3

--- a/solution.py
+++ b/solution.py
@@ -150,7 +150,7 @@
 
     for step in range(1, LINE):
 
-        @pl.when(ahead(step) < shards)
+        @pl.when(place + step < LINE)
         def _():
             for chunk in range(CHUNKS):
                 block_send(step, ahead(step), chunk).start()
@@ -206,6 +206,13 @@
             part = dot_nn(low, vals)
             acc[rows, 0:width] = acc[rows, 0:width] * shrink + part[:, 0:width]
             acc[rows, width:] = acc[rows, width:] * shrink + part[:, width:]
+
+    for step in range(1, LINE):
+
+        @pl.when(jnp.logical_and(place + step >= LINE, ahead(step) < shards))
+        def _():
+            for chunk in range(CHUNKS):
+                block_send(step, ahead(step), chunk).start()
 
     score_pass(0, True)
     for h in range(heads):

time: 52.3 us -> 52.3 us (level)
  no operation moved by 1% of the time
where the time goes in v4:
time: 52.3 us; the launch traced here: 52.2 us
  Pallas kernels  51.6 us (99%)
  between operations  0.64 us (1%)
    pallas_call x1, Pallas kernels, on_device(): pl.pallas_call(functools.partial(kernel, shards, lengths.shape[0]), out_s...  49.7 us
    pallas_call x1, Pallas kernels, on_device(): pl.pallas_call(hand_on, out_shape=tuple((jax.ShapeDtypeStruct(r.shape, r....  1.88 us

profile of v4, /device:TPU:97, one launch (start us, length us, event | category | flops | bytes accessed | tf_op | source)
XLA Modules:
  0.0 52.2 jit_solution(15316821487125214865)
XLA Ops:
  0.6 49.7 %packed_attention.1 = (bf16[512,256]{1,0:T(8,128)(2,1)}, bf16[512,256]{1,0:T(8,128)(2,1)}, bf16[256,128]{1,0:T(8,128)(2,1)}, bf16[256,128]{1,0:T(8,128)(2,1)}) custom-call(s32[64]{0:T(128)} %len_ref.1, bf16[512,256]{1,0:T(8,128)(2,1)} %q_hbm.1, bf16[512,128]{1,0:T(8,128)(2,1)} %k_hbm.1, bf16[512,128]{1,0:T(8,128)(2,1)} %v_hbm.1, bf16[512,256]{1,0:T(8,128)(2,1)} %g_hbm.1), custom_call_target="tpu_custom_call" | custom-call | flops 6442450944 | bytes 2097152 | tf_op jit(solution)/shard_map/packed_attention/pallas_call | solution.py:442
  50.3 1.9 %hand_on.1 = (bf16[512,256]{1,0:T(8,128)(2,1)}, bf16[512,256]{1,0:T(8,128)(2,1)}, bf16[256,128]{1,0:T(8,128)(2,1)}, bf16[256,128]{1,0:T(8,128)(2,1)}) custom-call(bf16[512,256]{1,0:T(8,128)(2,1)} %get-tuple-element.8.refs_0_, bf16[512,256]{1,0:T(8,128)(2,1)} %get-tuple-element.9.refs_1_, bf16[256,128]{1,0:T(8,128)(2,1)} %get-tuple-element.10.refs_2_, ...), custom_call_target="tpu_custom_call" | custom-call | tf_op jit(solution)/shard_map/hand_on/pallas_call | solution.py:485
